TPU v7x, 512 devices: a whole 4x4x16 slice. The times are simulated.
512 devices in a mesh: index: 16 (over z), head: 32 (over x, y, core).
Axes of the slice: x: 4, y: 4, z: 16, core: 2. Of those that a mesh axis runs over, the one named last changes fastest.
Arguments:
- queries: bfloat16 [4096, 4096], P('head'), may hold values from -32 to 32
- local_read: bfloat16 [4096, 4096], P(('index', 'head')), may hold values from -1.5 to 1.5
- gate_logits: float32 [32], replicated, may hold values from -2 to 2
- memory_keys: bfloat16 [16, 32, 4096, 128], P('index', 'head'), may hold values from -32 to 32
- memory_values: bfloat16 [16, 32, 4096, 128], P('index', 'head'), may hold values from -8 to 8
- probe_blocks: int32 [16, 32, 16], P('index', 'head'), may hold values from 0 to 31
- probe_counts: int32 [16, 32], P('index', 'head'), may hold values from 1 to 16, 256 in all within a row
Outputs:
- layer_read: bfloat16 [4096, 4096], P(('index', 'head'))
Inputs may be any that keep to these rules, and one draw needn't show every extreme that they name: `probe_counts`: in each group the counts over heads sum to 256.
All inputs are finite; a program needn't handle non-finite values.
Results may differ from a plain program's by a relative error of at most 0.0041.
Values may be sent and summed in bfloat16 or wider, within the bound.
A program may use at most 64 MiB of HBM per device.

v0:
```python
import jax
import jax.numpy as jnp
from jax import lax
from jax.sharding import PartitionSpec as P

DH = 128
BLOCK = 128
PMAX = 16


def slab_partials(head_queries, key_slab, value_slab, blocks, live_count):
    head_width = key_slab.shape[-1]
    offsets = jnp.arange(BLOCK, dtype=jnp.int32)
    row_ids = (blocks[:, None] * BLOCK + offsets[None, :]).reshape(-1)
    picked_keys = jnp.take(key_slab, row_ids, axis=0)
    picked_values = jnp.take(value_slab, row_ids, axis=0)
    usable = jnp.repeat(jnp.arange(PMAX, dtype=jnp.int32) < live_count, BLOCK)
    row_count = head_queries.shape[0]
    block_len = min(512, row_count)
    blocked = head_queries.reshape(row_count // block_len, block_len, head_width)

    def one_block(block_rows):
        scores = lax.dot_general(
            block_rows, picked_keys, (((1,), (1,)), ((), ())), preferred_element_type=jnp.float32
        ) * head_width ** (-0.5)
        scores = jnp.where(usable[None, :], scores, -jnp.inf)
        maxima = jnp.max(scores, axis=1)
        weights = jnp.exp(scores - maxima[:, None])
        totals = jnp.sum(weights, axis=1)
        weighted = jnp.dot(
            weights.astype(jnp.bfloat16), picked_values, preferred_element_type=jnp.float32
        )
        return (maxima, totals, weighted)

    maxima, totals, weighted = lax.map(one_block, blocked)
    return (
        maxima.reshape(row_count),
        totals.reshape(row_count),
        weighted.reshape(row_count, head_width),
    )


def local(queries, local_read, gate_logits, memory_keys, memory_values, probe_blocks, probe_counts):
    by_head = lax.all_to_all(queries, "head", split_axis=1, concat_axis=0, tiled=True)
    maxima, totals, weighted = slab_partials(
        by_head, memory_keys[0, 0], memory_values[0, 0], probe_blocks[0, 0], probe_counts[0, 0]
    )
    group_maxima, group_totals, group_weighted = (
        lax.all_to_all(maxima[None], "index", split_axis=1, concat_axis=0, tiled=True),
        lax.all_to_all(totals[None], "index", split_axis=1, concat_axis=0, tiled=True),
        lax.all_to_all(weighted[None], "index", split_axis=1, concat_axis=0, tiled=True),
    )
    highest = jnp.max(group_maxima, axis=0)
    factor = jnp.exp(group_maxima - highest[None])
    denominator = jnp.sum(group_totals * factor, axis=0)
    numerator = jnp.sum(group_weighted * factor[..., None], axis=0)
    memory_read = (numerator / denominator[..., None]).astype(jnp.bfloat16)
    returned = lax.all_to_all(memory_read, "head", split_axis=0, concat_axis=1, tiled=True)
    opening = jnp.repeat(jax.nn.sigmoid(gate_logits), DH)
    mixed = opening * returned.astype(jnp.float32) + (1.0 - opening) * local_read.astype(
        jnp.float32
    )
    return mixed.astype(jnp.bfloat16)


def solution(mesh):
    return jax.shard_map(
        local,
        mesh=mesh,
        in_specs=(
            P("head", None),
            P(("index", "head"), None),
            P(),
            P("index", "head", None, None),
            P("index", "head", None, None),
            P("index", "head", None),
            P("index", "head"),
        ),
        out_specs=P(("index", "head"), None),
        check_vma=False,
    )
```

profile of v0, /device:TPU:7, one launch (start us, length us, event | category | flops | bytes accessed | tf_op | source)
XLA Modules:
  0.0 210.8 jit_solution(6113717226698104430)
XLA Ops:
  0.0 2.7 %copy_bitcast_fusion = bf16[128,32,128]{2,0,1:T(8,128)(2,1)} fusion(bf16[128,4096]{1,0:T(8,128)(2,1)} %param.11), kind=kLoop, calls=%fused_computation.20 | loop fusion | bytes 2097152 | tf_op jit(solution)/shard_map/all_to_all | solution.py:44
  2.7 9.9 %all-to-all-start = ((bf16[128,32,128]{2,0,1:T(8,128)(2,1)}), bf16[128,32,128]{2,0,1:T(8,128)(2,1)S(1)}, u32[]{:S(2)}, u32[]{:S(2)}) async-start(bf16[128,32,128]{2,0,1:T(8,128)(2,1)} %copy_bitcast_fusion), calls=%async_computation | async-start | bytes 2097152 | tf_op jit(solution)/shard_map/all_to_all | solution.py:44
  12.7 8.1 %gather_fusion = bf16[2048,128]{1,0:T(8,128)(2,1)} fusion(bf16[4096,128]{1,0:T(8,128)(2,1)S(1)} %bitcast.81, s32[2048]{0:T(1024)S(1)} %fusion.25), kind=kCustom, calls=%fused_computation.clone | custom fusion | bytes 1056768 | tf_op jit(solution)/shard_map/jit(_take)/gather | solution.py:15
  20.8 8.0 %gather_fusion.1 = bf16[2048,128]{1,0:T(8,128)(2,1)} fusion(bf16[4096,128]{1,0:T(8,128)(2,1)S(1)} %bitcast.82, s32[2048]{0:T(1024)S(1)} %fusion.25), kind=kCustom, calls=%fused_computation.1.clone | custom fusion | bytes 1056768 | tf_op jit(solution)/shard_map/jit(_take)/gather | solution.py:16
  29.5 1.5 broadcast_select_fusion
  31.0 29.3 %while.15 = (s32[]{:T(128)}, f32[8,512]{1,0:T(8,128)S(1)}, f32[8,512]{1,0:T(8,128)S(1)}, f32[8,512,128]{2,1,0:T(8,128)}, bf16[8,512,128]{2,1,0:T(8,128)(2,1)S(1)...) while((s32[]{:T(128)}, f32[8,512]{1,0:T(8,128)S(1)}, ...), condition=%wide.region_3.5_spmd.clone, body=%wide.region_0.4_spmd.clone.sunk | while | flops 548404224 | bytes 14049921 | solution.py:35
  32.0 1.7 fusion.44
  35.6 1.7 fusion.44
  37.3 0.9 fusion.43
  39.3 1.7 fusion.44
  41.0 0.9 fusion.43
  42.9 1.7 fusion.44
  44.6 0.9 fusion.43
  46.6 1.7 fusion.44
  50.3 1.7 fusion.44
  54.0 1.7 fusion.44
  57.6 1.7 fusion.44
  61.0 12.9 %all-to-all-start.2 = ((f32[1,16,256]{2,0,1:T(1,128)}), f32[1,16,256]{2,0,1:T(1,128)S(1)}, u32[]{:S(2)}, u32[]{:S(2)}) async-start(f32[1,16,256]{2,0,1:T(1,128)} %all_to_all.58), calls=%async_computation.2 | async-start | bytes 32768 | tf_op jit(solution)/shard_map/all_to_all | solution.py:49
  74.0 11.4 %all-to-all-done.2 = f32[1,16,256]{2,0,1:T(1,128)S(1)} async-done(((f32[1,16,256]{2,0,1:T(1,128)}), f32[1,16,256]{2,0,1:T(1,128)S(1)}, u32[]{:S(2)}, u32[]{:S(2)}) %all-to-all-start.2) | async-done | bytes 16416 | tf_op jit(solution)/shard_map/all_to_all | solution.py:49
  85.4 13.8 %all_to_all.70 = f32[1,16,256]{2,0,1:T(1,128)S(1)} all-to-all(f32[1,16,256]{2,0,1:T(1,128)S(1)} %all_to_all.61), channel_id=1, replica_groups=mesh['index'=16,'head'=32] {'index'}, dimensions={1} | all-to-all | bytes 32768 | tf_op jit(solution)/shard_map/all_to_all | solution.py:50
  99.2 3.7 %all-to-all-start.1 = ((f32[1,4096,128]{2,0,1:T(1,128)}), f32[1,4096,128]{2,0,1:T(1,128)S(1)}, u32[]{:S(2)}, u32[]{:S(2)}) async-start(f32[1,4096,128]{2,0,1:T(1,128)} %bitcast.8), calls=%async_computation.1 | async-start | bytes 4194304 | tf_op jit(solution)/shard_map/all_to_all | solution.py:51
  103.1 91.5 %all-to-all-done.1 = f32[1,4096,128]{2,0,1:T(1,128)S(1)} async-done(((f32[1,4096,128]{2,0,1:T(1,128)}), f32[1,4096,128]{2,0,1:T(1,128)S(1)}, u32[]{:S(2)}, u32[]{:S(2)}) %all-to-all-start.1) | async-done | bytes 2097184 | tf_op jit(solution)/shard_map/all_to_all | solution.py:51
  196.1 8.5 %all-to-all-start.4 = ((bf16[32,8,128]{2,1,0:T(8,128)(2,1)}), bf16[32,8,128]{2,1,0:T(8,128)(2,1)S(1)}, u32[]{:S(2)}, u32[]{:S(2)}) async-start(bf16[32,8,128]{2,1,0:T(8,128)(2,1)} %fusion.22), calls=%async_computation.4 | async-start | bytes 131072 | tf_op jit(solution)/shard_map/all_to_all | solution.py:58
  204.6 5.5 %all-to-all-done.4 = bf16[32,8,128]{2,1,0:T(8,128)(2,1)S(1)} async-done(((bf16[32,8,128]{2,1,0:T(8,128)(2,1)}), bf16[32,8,128]{2,1,0:T(8,128)(2,1)S(1)}, u32[]{:S(2)}, u32[]{:S(2)}) %all-to-all-start.4) | async-done | bytes 65568 | tf_op jit(solution)/shard_map/all_to_all | solution.py:58
  (66 shorter events, 16.0 us)
Async XLA Ops:
  0.0 12.7 %copy-start = (bf16[1,1,4096,128]{3,2,1,0:T(8,128)(2,1)S(1)}, bf16[1,1,4096,128]{3,2,1,0:T(8,128)(2,1)}, u32[]{:S(2)}) copy-start(bf16[1,1,4096,128]{3,2,1,0:T(8,128)(2,1)} %param.14) | copy-start | bytes 3145732
  0.0 12.6 %copy-start.3 = (s32[1,1,16]{2,1,0:T(1,128)S(1)}, s32[1,1,16]{2,1,0:T(1,128)}, u32[]{:S(2)}) copy-start(s32[1,1,16]{2,1,0:T(1,128)} %param.16) | copy-start | bytes 196
  0.0 20.8 %copy-start.1 = (bf16[1,1,4096,128]{3,2,1,0:T(8,128)(2,1)S(1)}, bf16[1,1,4096,128]{3,2,1,0:T(8,128)(2,1)}, u32[]{:S(2)}) copy-start(bf16[1,1,4096,128]{3,2,1,0:T(8,128)(2,1)} %param.15) | copy-start | bytes 3145732
  2.7 28.4 %all-to-all-start = ((bf16[128,32,128]{2,0,1:T(8,128)(2,1)}), bf16[128,32,128]{2,0,1:T(8,128)(2,1)S(1)}, u32[]{:S(2)}, u32[]{:S(2)}) async-start(bf16[128,32,128]{2,0,1:T(8,128)(2,1)} %copy_bitcast_fusion), calls=%async_computation | async-start | bytes 2097152 | tf_op jit(solution)/shard_map/all_to_all | solution.py:44
  60.4 42.5 %copy-start.4 = (f32[32]{0:T(128)S(1)}, f32[32]{0:T(128)}, u32[]{:S(2)}) copy-start(f32[32]{0:T(128)} %param.13) | copy-start | bytes 388
  60.4 149.7 %copy-start.2 = (bf16[8,4096]{1,0:T(8,128)(2,1)S(1)}, bf16[8,4096]{1,0:T(8,128)(2,1)}, u32[]{:S(2)}) copy-start(bf16[8,4096]{1,0:T(8,128)(2,1)} %param.12) | copy-start | bytes 196612
  61.0 24.3 %all-to-all-start.2 = ((f32[1,16,256]{2,0,1:T(1,128)}), f32[1,16,256]{2,0,1:T(1,128)S(1)}, u32[]{:S(2)}, u32[]{:S(2)}) async-start(f32[1,16,256]{2,0,1:T(1,128)} %all_to_all.58), calls=%async_computation.2 | async-start | bytes 32768 | tf_op jit(solution)/shard_map/all_to_all | solution.py:49
  99.2 95.4 %all-to-all-start.1 = ((f32[1,4096,128]{2,0,1:T(1,128)}), f32[1,4096,128]{2,0,1:T(1,128)S(1)}, u32[]{:S(2)}, u32[]{:S(2)}) async-start(f32[1,4096,128]{2,0,1:T(1,128)} %bitcast.8), calls=%async_computation.1 | async-start | bytes 4194304 | tf_op jit(solution)/shard_map/all_to_all | solution.py:51
  196.1 14.1 %all-to-all-start.4 = ((bf16[32,8,128]{2,1,0:T(8,128)(2,1)}), bf16[32,8,128]{2,1,0:T(8,128)(2,1)S(1)}, u32[]{:S(2)}, u32[]{:S(2)}) async-start(bf16[32,8,128]{2,1,0:T(8,128)(2,1)} %fusion.22), calls=%async_computation.4 | async-start | bytes 131072 | tf_op jit(solution)/shard_map/all_to_all | solution.py:58
where the time goes:
time: 214 us; the launch traced here: 211 us
  waiting for transfers between devices  108 us (50%)
  starting transfers between devices  35 us (16%)
  local copies, waits for them, and re-layouts  21.1 us (10%)
  matrix products  20.1 us (9%)
  blocking collectives  13.8 us (6%)
  other arithmetic  11.4 us (5%)
    all_to_all x1, waiting for transfers between devices, local(): lax.all_to_all(weighted[None], 'index', split_axis=1, concat_axis=0, tile...  91.5 us
    all_to_all x1, blocking collectives, local(): lax.all_to_all(totals[None], 'index', split_axis=1, concat_axis=0, tiled=...  13.8 us
    dot_general x8, matrix products, one_block(): jnp.dot(weights.astype(jnp.bfloat16), picked_values, preferred_element_ty...  13.5 us
    all_to_all x1, starting transfers between devices, local(): lax.all_to_all(maxima[None], 'index', split_axis=1, concat_axis=0, tiled=...  12.9 us
    all_to_all x1, waiting for transfers between devices, local(): lax.all_to_all(maxima[None], 'index', split_axis=1, concat_axis=0, tiled=...  11.4 us
    all_to_all x1, starting transfers between devices, local(): lax.all_to_all(queries, 'head', split_axis=1, concat_axis=0, tiled=True)  9.9 us
    all_to_all x1, starting transfers between devices, local(): lax.all_to_all(memory_read, 'head', split_axis=0, concat_axis=1, tiled=True)  8.49 us
    gather x1, local copies, waits for them, and re-layouts, slab_partials(): picked_keys = jnp.take(key_slab, row_ids, axis=0)  8.05 us
  transfers between devices with their start and end apart: 4, of which 3 were waited for; matrix products, arithmetic and copies ran while one was open for 9% of the time, Pallas kernels for 0%

commit v1 on v0

v1 whole, which is shorter than its diff:
```python
import functools
import math

import jax
import jax.numpy as jnp
from jax import lax
from jax.experimental import pallas as pl
from jax.experimental.pallas import tpu as pltpu
from jax.sharding import PartitionSpec as P

DH = 128
BLOCK = 128
PMAX = 16
GROUPS = 16
HEADS = 32
KEYS = PMAX * BLOCK
SCALE = DH ** -0.5 * math.log2(math.e)
MESH = pl.DeviceIdType.MESH

PHASES = 2
ROUNDS = 4
PART = 128 // PHASES
CHUNK = 2 * PART
TILE = 256
VROWS = 144
MSG = 144
NEUTRAL = -1e30


def add(a, b):
    return b if a is None else a + b


def load_message(ref):
    o = ref[0:DH, :].astype(jnp.float32)
    stats = ref[DH:MSG, :].astype(jnp.float32)
    m = stats[0:1] + stats[1:2] + stats[2:3]
    l = stats[3:4] + stats[4:5] + stats[5:6]
    return o, m, l


def pieces(x):
    hi = x.astype(jnp.bfloat16).astype(jnp.float32)
    rest = x - hi
    mid = rest.astype(jnp.bfloat16).astype(jnp.float32)
    return hi, mid, rest - mid


def store_message(ref, o, m, l):
    ref[0:DH, :] = o.astype(ref.dtype)
    row = lax.broadcasted_iota(jnp.int32, (MSG - DH, CHUNK), 0)
    stats = jnp.zeros((MSG - DH, CHUNK), jnp.float32)
    for i, piece in enumerate(pieces(m) + pieces(l)):
        stats = jnp.where(row == i, piece, stats)
    ref[DH:MSG, :] = stats.astype(ref.dtype)


def merge(parts):
    top = parts[0][1]
    for _, m, _ in parts[1:]:
        top = jnp.maximum(top, m)
    o = l = None
    for po, pm, pn in parts:
        factor = jnp.exp2((pm - top) * SCALE)
        o = add(o, po * factor)
        l = add(l, pn * factor)
    return o, top, l


def kernel(
    blocks_ref, count_ref, q_ref, k_ref, v_ref, read_ref,
    qa, kp, vt, scores, own_o, own_s, out_buf, in_buf, result,
    q_send, q_recv, m_send, m_recv, r_send, r_recv,
):
    g = lax.axis_index("index")
    h = lax.axis_index("head")

    def plane(step):
        return lax.rem(g + step + 2 * GROUPS, GROUPS)

    barrier = pltpu.get_barrier_semaphore()

    def greet(i, _):
        pl.semaphore_signal(barrier, inc=1, device_id=(g, lax.rem(h + i, HEADS)), device_id_type=MESH)
        return 0

    lax.fori_loop(1, HEADS, greet, 0)
    for step in (-2, -1, 1, 2):
        pl.semaphore_signal(barrier, inc=1, device_id=(plane(step), h), device_id_type=MESH)
    pl.semaphore_wait(barrier, HEADS - 1 + 4)

    for p in range(PHASES):

        def send_rows(i, _):
            to = lax.rem(h + i, HEADS)
            pltpu.make_async_remote_copy(
                src_ref=q_ref.at[pl.ds(p * PART, PART), pl.ds(pl.multiple_of(to * DH, DH), DH)],
                dst_ref=qa.at[p, pl.ds(pl.multiple_of(h * PART, PART), PART), :],
                send_sem=q_send.at[p],
                recv_sem=q_recv.at[p],
                device_id=(g, to),
                device_id_type=MESH,
            ).start()
            return 0

        lax.fori_loop(1, HEADS, send_rows, 0)
        qa[p, pl.ds(pl.multiple_of(h * PART, PART), PART), :] = q_ref[
            pl.ds(p * PART, PART), pl.ds(pl.multiple_of(h * DH, DH), DH)
        ]

    def wait_rows(p):
        part = qa.at[p, pl.ds(0, (HEADS - 1) * PART), :]
        pltpu.make_async_copy(part, part, q_recv.at[p]).wait()

    count = count_ref[0, 0]
    first = blocks_ref[0, 0, 0]
    row = lax.broadcasted_iota(jnp.int32, (VROWS - DH, BLOCK), 0)
    for j in range(PMAX):
        live = lax.div(count + (PMAX - 1 - j), PMAX)
        block = first + live * (blocks_ref[0, 0, j] - first)
        span = pl.ds(j * BLOCK, BLOCK)
        kp[span, :] = k_ref[block]
        gain = live.astype(jnp.float32)
        values = v_ref[block].astype(jnp.float32) * gain
        vt[0:DH, span] = values.T.astype(jnp.bfloat16)
        vt[DH:VROWS, span] = jnp.where(row == 0, gain, 0.0).astype(jnp.bfloat16)

    def blank(slot):
        zero = jnp.zeros((DH, CHUNK), jnp.float32)
        line = jnp.zeros((1, CHUNK), jnp.float32)
        store_message(slot, zero, line + NEUTRAL, line)

    for p in range(PHASES):
        blank(in_buf.at[0, p, 0])
        blank(in_buf.at[1, p, 0])
        blank(in_buf.at[2, p, 0])
        blank(in_buf.at[2, p, 1])
        blank(in_buf.at[3, p, 0])

    hop = (2, 1, -2, -1)

    def message(kind, p, r):
        return pltpu.make_async_remote_copy(
            src_ref=out_buf.at[kind, p, r],
            dst_ref=in_buf.at[kind, p, r + 1],
            send_sem=m_send.at[kind, p, r],
            recv_sem=m_recv.at[kind, p, r],
            device_id=(plane(hop[kind]), h),
            device_id_type=MESH,
        )

    def arrived(kind, p, r):
        message(kind, p, r).wait_recv()

    def schedule(i):
        p = 1 - lax.rem(i, 2) + lax.div(i, 7) - lax.div(7 - i, 7)
        r = (1 - p) * lax.div(i + 1, 2) + p * (lax.div(i, 2) - 1 + lax.div(i, 7))
        return p, r

    def rows_of(p, step):
        return qa[p, pl.ds(pl.multiple_of(plane(step) * CHUNK, CHUNK), CHUNK), :]

    def right_rows(p, r):
        return jnp.concatenate([rows_of(p, 8 - 2 * r), rows_of(p, 7 - 2 * r)], axis=0)

    def left_rows(p, r):
        even = (8 - 2 * r) * lax.div(r + 3, 4)
        return jnp.concatenate([rows_of(p, -even), rows_of(p, 2 * r - 7)], axis=0)

    def score_tile(q, slot, k):
        s = lax.dot_general(
            kp[k : k + TILE, :], q, (((1,), (1,)), ((), ())), preferred_element_type=jnp.float32
        )
        scores[slot, k : k + TILE, :] = s
        return jnp.max(s.reshape(TILE // 8, 8, 2 * CHUNK), axis=0)

    def value_tile(slot, m, k):
        w = jnp.exp2((scores[slot, k : k + TILE, :] - m) * SCALE).astype(jnp.bfloat16)
        return jnp.dot(vt[:, k : k + TILE], w, preferred_element_type=jnp.float32)

    def unit(q_next, m, slot):
        top = acc = None
        for k in range(0, KEYS, TILE):
            t = score_tile(q_next, 1 - slot, k)
            top = t if top is None else jnp.maximum(top, t)
            acc = add(acc, value_tile(slot, m, k))
        return acc, jnp.max(top, axis=0, keepdims=True)

    def halves(acc, m):
        even = (acc[0:DH, 0:CHUNK], m[:, 0:CHUNK], acc[DH : DH + 1, 0:CHUNK])
        odd = (acc[0:DH, CHUNK:], m[:, CHUNK:], acc[DH : DH + 1, CHUNK:])
        return even, odd

    def received(kind, p, slot):
        return load_message(in_buf.at[kind, p, slot])

    wait_rows(0)
    q = right_rows(0, 0)
    top = None
    for k in range(0, KEYS, TILE):
        t = score_tile(q, 0, k)
        top = t if top is None else jnp.maximum(top, t)
    top = jnp.max(top, axis=0, keepdims=True)

    def body(i, m_right):
        p, r = schedule(i)
        acc, m_left = unit(left_rows(p, r), m_right, 0)
        even, odd = halves(acc, m_right)
        store_message(out_buf.at[1, p, r], *odd)
        message(1, p, r).start()

        @pl.when(r > 0)
        def _():
            arrived(0, p, r - 1)
            arrived(1, p, r - 1)

        store_message(out_buf.at[0, p, r], *merge([received(0, p, r), received(1, p, r), even]))
        message(0, p, r).start()

        @pl.when(i == 1)
        def _():
            wait_rows(1)

        pn, rn = schedule(i + 1 - lax.div(i + 1, 8))
        acc, m_next = unit(right_rows(pn, rn), m_left, 1)
        even, odd = halves(acc, m_left)
        store_message(out_buf.at[3, p, r], *odd)
        message(3, p, r).start()

        @pl.when(r == 0)
        def _():
            own_o[p] = even[0]
            own_s[p, 0:1] = even[1]
            own_s[p, 1:2] = even[2]

        @pl.when(r > 0)
        def _():
            arrived(3, p, r - 1)

            @pl.when(r > 1)
            def _():
                arrived(2, p, r - 1)

            store_message(out_buf.at[2, p, r], *merge([received(2, p, r), received(3, p, r), even]))
            message(2, p, r).start()

        return m_next

    lax.fori_loop(0, PHASES * ROUNDS, body, top)

    for p in range(PHASES):
        for kind in range(4):
            arrived(kind, p, ROUNDS - 1)
        parts = [received(kind, p, ROUNDS) for kind in range(4)]
        parts.append((own_o[p], own_s[p, 0:1], own_s[p, 1:2]))
        o, _, l = merge(parts)
        read = (o / l).T.astype(jnp.bfloat16).astype(jnp.float32)
        result[p] = read

        def give(b, _):
            to = lax.div(b, 8) * 16 + 8 * p + lax.rem(b, 8)

            @pl.when(to != h)
            def _():
                pltpu.make_async_remote_copy(
                    src_ref=result.at[p, pl.ds(pl.multiple_of(b * 8, 8), 8), :],
                    dst_ref=read_ref.at[:, pl.ds(pl.multiple_of(h * DH, DH), DH)],
                    send_sem=r_send,
                    recv_sem=r_recv,
                    device_id=(g, to),
                    device_id_type=MESH,
                ).start()

            @pl.when(to == h)
            def _():
                read_ref[:, pl.ds(pl.multiple_of(h * DH, DH), DH)] = result[
                    p, pl.ds(pl.multiple_of(b * 8, 8), 8), :
                ]

            return 0

        lax.fori_loop(0, 16, give, 0)

    for p in range(PHASES):
        part = qa.at[p, pl.ds(0, (HEADS - 1) * PART), :]
        pltpu.make_async_copy(part, part, q_send.at[p]).wait()
        for kind in range(4):
            for r in range(ROUNDS):
                if kind == 2 and r == 0:
                    continue
                message(kind, p, r).wait_send()
    span = read_ref.at[:, pl.ds(0, (HEADS - 1) * DH)]
    pltpu.make_async_copy(span, span, r_send).wait()
    pltpu.make_async_copy(span, span, r_recv).wait()


def memory_reads(queries, memory_keys, memory_values, probe_blocks, probe_counts):
    vmem = pl.BlockSpec(memory_space=pltpu.VMEM)
    smem = pl.BlockSpec(memory_space=pltpu.SMEM)
    return pl.pallas_call(
        kernel,
        out_shape=jax.ShapeDtypeStruct((8, HEADS * DH), jnp.float32),
        in_specs=[smem, smem, vmem, vmem, vmem],
        out_specs=vmem,
        scratch_shapes=[
            pltpu.VMEM((PHASES, HEADS * PART, DH), jnp.bfloat16),
            pltpu.VMEM((KEYS, DH), jnp.bfloat16),
            pltpu.VMEM((VROWS, KEYS), jnp.bfloat16),
            pltpu.VMEM((2, KEYS, 2 * CHUNK), jnp.float32),
            pltpu.VMEM((PHASES, DH, CHUNK), jnp.float32),
            pltpu.VMEM((PHASES, 8, CHUNK), jnp.float32),
            pltpu.VMEM((4, PHASES, ROUNDS, MSG, CHUNK), jnp.bfloat16),
            pltpu.VMEM((4, PHASES, ROUNDS + 1, MSG, CHUNK), jnp.bfloat16),
            pltpu.VMEM((PHASES, CHUNK, DH), jnp.float32),
            pltpu.SemaphoreType.DMA((PHASES,)),
            pltpu.SemaphoreType.DMA((PHASES,)),
            pltpu.SemaphoreType.DMA((4, PHASES, ROUNDS)),
            pltpu.SemaphoreType.DMA((4, PHASES, ROUNDS)),
            pltpu.SemaphoreType.DMA,
            pltpu.SemaphoreType.DMA,
        ],
        compiler_params=pltpu.CompilerParams(
            collective_id=0, has_side_effects=True, vmem_limit_bytes=48 << 20
        ),
        name="memory_reads",
    )(
        probe_blocks,
        probe_counts,
        queries,
        memory_keys.reshape(-1, BLOCK, DH),
        memory_values.reshape(-1, BLOCK, DH),
    )


def local(queries, local_read, gate_logits, memory_keys, memory_values, probe_blocks, probe_counts):
    reads = memory_reads(queries, memory_keys, memory_values, probe_blocks, probe_counts)
    opening = jnp.repeat(jax.nn.sigmoid(gate_logits), DH)
    mixed = opening * reads + (1.0 - opening) * local_read.astype(jnp.float32)
    return mixed.astype(jnp.bfloat16)


def solution(mesh):
    return jax.shard_map(
        local,
        mesh=mesh,
        in_specs=(
            P("head", None),
            P(("index", "head"), None),
            P(),
            P("index", "head", None, None),
            P("index", "head", None, None),
            P("index", "head", None),
            P("index", "head"),
        ),
        out_specs=P(("index", "head"), None),
        check_vma=False,
    )
```

time: 214 us -> 65.7 us (0.31); the launches traced: 211 us -> 65.4 us
  waiting for transfers between devices: 108 us -> 0 us
  Pallas kernels: 0 us -> 59 us
  starting transfers between devices: 35 us -> 0 us
  matrix products: 20.1 us -> 0 us
  local copies, waits for them, and re-layouts: 21.1 us -> 4.99 us
  blocking collectives: 13.8 us -> 0 us
  other arithmetic: 11.4 us -> 0.74 us
    all_to_all x4 -> x0, waiting for transfers between devices: 108 us -> none  [the longest x1 91.5 us: local(): lax.all_to_all(weighted[None], 'index', split_axis=1, concat_axis=0, tile...]
    pallas_call x0 -> x1, Pallas kernels: none -> 59 us  [memory_reads(): pl.pallas_call(kernel, out_shape=jax.ShapeDtypeStruct((8, HEADS * DH), jn...]
    all_to_all x4 -> x0, starting transfers between devices: 35 us -> none  [the longest x1 12.9 us: local(): lax.all_to_all(maxima[None], 'index', split_axis=1, concat_axis=0, tiled=...]
    dot_general x16 -> x0, matrix products: 20.1 us -> none  [the longest x8 13.5 us: one_block(): jnp.dot(weights.astype(jnp.bfloat16), picked_values, preferred_element_ty...]
    gather x2 -> x0, local copies, waits for them, and re-layouts: 16.1 us -> none  [the longest x1 8.05 us: slab_partials(): picked_keys = jnp.take(key_slab, row_ids, axis=0)]
    all_to_all x1 -> x0, blocking collectives: 13.8 us -> none  [local(): lax.all_to_all(totals[None], 'index', split_axis=1, concat_axis=0, tiled=...]
    reduce_sum x10 -> x0, other arithmetic: 8.21 us -> none  [the longest x8 7.48 us: one_block(): totals = jnp.sum(weights, axis=1)]
    unnamed x10 -> x12, local copies, waits for them, and re-layouts: 0.02 us -> 4.92 us
  transfers between devices with their start and end apart: 4 -> 0, of which waited for: 3 -> 0; matrix products, arithmetic and copies ran while one was open for 9% -> 0% of each run, Pallas kernels for 0% -> 0%
where the time goes in v1:
time: 65.7 us; the launch traced here: 65.4 us
  Pallas kernels  59 us (90%)
  local copies, waits for them, and re-layouts  4.99 us (8%)
  other arithmetic  0.74 us (1%)
  between operations  0.68 us (1%)
    pallas_call x1, Pallas kernels, memory_reads(): pl.pallas_call(kernel, out_shape=jax.ShapeDtypeStruct((8, HEADS * DH), jn...  59 us
    unnamed x12, local copies, waits for them, and re-layouts  4.92 us

profile of v1, /device:TPU:7, one launch (start us, length us, event | category | flops | bytes accessed | tf_op | source)
XLA Modules:
  0.0 65.4 jit_solution(6767350664261394897)
XLA Ops:
  0.7 0.0 copy-start.5
  0.7 0.6 copy-done.5
  1.3 0.1 bitcast_subtract_fusion
  1.4 0.0 copy-start.3
  1.4 0.1 broadcast_bitcast_fusion
  1.5 0.6 copy-done.3
  2.1 0.0 copy-start
  2.1 1.2 %copy-done = bf16[128,4096]{1,0:T(8,128)(2,1)S(1)} copy-done((bf16[128,4096]{1,0:T(8,128)(2,1)S(1)}, bf16[128,4096]{1,0:T(8,128)(2,1)}, u32[]{:S(2)}) %copy-start) | copy-done | bytes 1048600
  3.3 0.0 copy-start.1
  3.3 1.2 %copy-done.1 = bf16[1,1,4096,128]{3,2,1,0:T(8,128)(2,1)S(1)} copy-done((bf16[1,1,4096,128]{3,2,1,0:T(8,128)(2,1)S(1)}, bf16[1,1,4096,128]{3,2,1,0:T(8,128)(2,1)}, u32[]{:S(2)}) %copy-start.1) | copy-done | bytes 1048600
  4.5 0.0 copy-start.2
  4.5 1.2 %copy-done.2 = bf16[1,1,4096,128]{3,2,1,0:T(8,128)(2,1)S(1)} copy-done((bf16[1,1,4096,128]{3,2,1,0:T(8,128)(2,1)S(1)}, bf16[1,1,4096,128]{3,2,1,0:T(8,128)(2,1)}, u32[]{:S(2)}) %copy-start.2) | copy-done | bytes 1048600
  5.7 0.0 copy-start.4
  5.7 59.0 %memory_reads.1 = f32[8,4096]{1,0:T(8,128)S(1)} custom-call(s32[1,1,16]{2,1,0:T(1,128)S(1)} %copy-done.3, s32[1,1]{1,0:T(1,128)S(6)} %copy.8.count_ref, bf16[128,4096]{1,0:T(8,128)(2,1)S(1)} %copy-done, bf16[32,128,128]{2,1,0:T(8,128)(2,1)S(1)} %bitcast.5, bf16[32,128,128]{2,1,0:T(8,128)(2,1)S(1)} %bitcast.6), custom_call_target="tpu_custom_call" | custom-call | tf_op jit(solution)/shard_map/memory_reads/pallas_call | solution.py:300
  64.8 0.0 copy-done.4
  64.8 0.7 %add_convert_fusion = bf16[8,4096]{1,0:T(8,128)(2,1)} fusion(bf16[8,4096]{1,0:T(8,128)(2,1)S(1)} %copy-done.4, f32[8,4096]{1,0:T(8,128)S(1)} %memory_reads.1, f32[4096]{0:T(1024)S(1)} %bitcast_subtract_fusion, f32[4096]{0:T(1024)S(1)} %broadcast_bitcast_fusion), kind=kLoop, calls=%fused_computation | loop fusion | flops 163840 | bytes 294912 | tf_op jit(solution)/shard_map/convert_element_type | solution.py:339
  (1 shorter events, 0.0 us)
Async XLA Ops:
  0.7 0.7 %copy-start.5 = (f32[32]{0:T(128)S(1)}, f32[32]{0:T(128)}, u32[]{:S(2)}) copy-start(f32[32]{0:T(128)} %param.9) | copy-start | bytes 388
  1.4 0.7 %copy-start.3 = (s32[1,1,16]{2,1,0:T(1,128)S(1)}, s32[1,1,16]{2,1,0:T(1,128)}, u32[]{:S(2)}) copy-start(s32[1,1,16]{2,1,0:T(1,128)} %blocks_ref.1) | copy-start | bytes 196
  2.1 1.2 %copy-start = (bf16[128,4096]{1,0:T(8,128)(2,1)S(1)}, bf16[128,4096]{1,0:T(8,128)(2,1)}, u32[]{:S(2)}) copy-start(bf16[128,4096]{1,0:T(8,128)(2,1)} %q_ref.1) | copy-start | bytes 3145732
  3.3 1.2 %copy-start.1 = (bf16[1,1,4096,128]{3,2,1,0:T(8,128)(2,1)S(1)}, bf16[1,1,4096,128]{3,2,1,0:T(8,128)(2,1)}, u32[]{:S(2)}) copy-start(bf16[1,1,4096,128]{3,2,1,0:T(8,128)(2,1)} %param.10) | copy-start | bytes 3145732
  4.5 1.2 %copy-start.2 = (bf16[1,1,4096,128]{3,2,1,0:T(8,128)(2,1)S(1)}, bf16[1,1,4096,128]{3,2,1,0:T(8,128)(2,1)}, u32[]{:S(2)}) copy-start(bf16[1,1,4096,128]{3,2,1,0:T(8,128)(2,1)} %param.11) | copy-start | bytes 3145732
  5.7 59.0 %copy-start.4 = (bf16[8,4096]{1,0:T(8,128)(2,1)S(1)}, bf16[8,4096]{1,0:T(8,128)(2,1)}, u32[]{:S(2)}) copy-start(bf16[8,4096]{1,0:T(8,128)(2,1)} %param.8) | copy-start | bytes 196612

commit v2 on v1

--- a/solution.py
+++ b/solution.py
@@ -24,7 +24,6 @@
 TILE = 256
 VROWS = 144
 MSG = 144
-NEUTRAL = -1e30
 
 
 def add(a, b):
@@ -68,15 +67,40 @@
 
 
 def kernel(
-    blocks_ref, count_ref, q_ref, k_ref, v_ref, read_ref,
-    qa, kp, vt, scores, own_o, own_s, out_buf, in_buf, result,
-    q_send, q_recv, m_send, m_recv, r_send, r_recv,
+    blocks_hbm, count_hbm, gate_hbm, q_ref, k_hbm, v_hbm, near_hbm, mixed_ref,
+    blocks_ref, count_ref, gate_ref, k_ref, v_ref, near_ref, opening, read_ref,
+    qa, kp, vt, scores, part_o, part_s, out_buf, in_buf, result,
+    load_sem, q_send, q_recv, m_send, m_recv, r_send, r_recv,
 ):
     g = lax.axis_index("index")
     h = lax.axis_index("head")
 
     def plane(step):
         return lax.rem(g + step + 2 * GROUPS, GROUPS)
+
+    own_rows = [
+        pltpu.make_async_copy(
+            q_ref.at[pl.ds(p * PART, PART), pl.ds(pl.multiple_of(h * DH, DH), DH)],
+            qa.at[p, pl.ds(pl.multiple_of(h * PART, PART), PART), :],
+            load_sem.at[p],
+        )
+        for p in range(PHASES)
+    ]
+    loads = [
+        pltpu.make_async_copy(src, dst, load_sem.at[PHASES + i])
+        for i, (src, dst) in enumerate(
+            (
+                (blocks_hbm, blocks_ref),
+                (count_hbm, count_ref),
+                (gate_hbm, gate_ref),
+                (k_hbm, k_ref),
+                (v_hbm, v_ref),
+                (near_hbm, near_ref),
+            )
+        )
+    ]
+    for copy in loads + own_rows:
+        copy.start()
 
     barrier = pltpu.get_barrier_semaphore()
 
@@ -104,14 +128,14 @@
             return 0
 
         lax.fori_loop(1, HEADS, send_rows, 0)
-        qa[p, pl.ds(pl.multiple_of(h * PART, PART), PART), :] = q_ref[
-            pl.ds(p * PART, PART), pl.ds(pl.multiple_of(h * DH, DH), DH)
-        ]
 
     def wait_rows(p):
+        own_rows[p].wait()
         part = qa.at[p, pl.ds(0, (HEADS - 1) * PART), :]
         pltpu.make_async_copy(part, part, q_recv.at[p]).wait()
 
+    for copy in loads:
+        copy.wait()
     count = count_ref[0, 0]
     first = blocks_ref[0, 0, 0]
     row = lax.broadcasted_iota(jnp.int32, (VROWS - DH, BLOCK), 0)
@@ -125,17 +149,9 @@
         vt[0:DH, span] = values.T.astype(jnp.bfloat16)
         vt[DH:VROWS, span] = jnp.where(row == 0, gain, 0.0).astype(jnp.bfloat16)
 
-    def blank(slot):
-        zero = jnp.zeros((DH, CHUNK), jnp.float32)
-        line = jnp.zeros((1, CHUNK), jnp.float32)
-        store_message(slot, zero, line + NEUTRAL, line)
-
-    for p in range(PHASES):
-        blank(in_buf.at[0, p, 0])
-        blank(in_buf.at[1, p, 0])
-        blank(in_buf.at[2, p, 0])
-        blank(in_buf.at[2, p, 1])
-        blank(in_buf.at[3, p, 0])
+    for j in range(HEADS):
+        logit = jnp.full((8, DH), gate_ref[j], jnp.float32)
+        opening[:, j * DH : (j + 1) * DH] = 1.0 / (1.0 + jnp.exp(-logit))
 
     hop = (2, 1, -2, -1)
 
@@ -152,9 +168,12 @@
     def arrived(kind, p, r):
         message(kind, p, r).wait_recv()
 
+    def from_step(i, a):
+        return lax.div(i + (8 - a), 8)
+
     def schedule(i):
-        p = 1 - lax.rem(i, 2) + lax.div(i, 7) - lax.div(7 - i, 7)
-        r = (1 - p) * lax.div(i + 1, 2) + p * (lax.div(i, 2) - 1 + lax.div(i, 7))
+        p = from_step(i, 3) - from_step(i, 5) + from_step(i, 6)
+        r = i - 3 * from_step(i, 3) + from_step(i, 5) - 2 * from_step(i, 6)
         return p, r
 
     def rows_of(p, step):
@@ -202,6 +221,25 @@
         top = t if top is None else jnp.maximum(top, t)
     top = jnp.max(top, axis=0, keepdims=True)
 
+    def keep(side, p, r, part):
+        part_o[side, p, r] = part[0]
+        part_s[side, p, r, 0:1] = part[1]
+        part_s[side, p, r, 1:2] = part[2]
+
+    def kept(side, p, r):
+        return part_o[side, p, r], part_s[side, p, r, 0:1], part_s[side, p, r, 1:2]
+
+    def pass_on(p, r):
+        for side in range(2):
+            parts = [kept(side, p, r)]
+            for kind in (2 * side, 2 * side + 1):
+                if kind == 2 and r == 1:
+                    continue
+                arrived(kind, p, r - 1)
+                parts.append(received(kind, p, r))
+            store_message(out_buf.at[2 * side, p, r], *merge(parts))
+            message(2 * side, p, r).start()
+
     def body(i, m_right):
         p, r = schedule(i)
         acc, m_left = unit(left_rows(p, r), m_right, 0)
@@ -209,15 +247,16 @@
         store_message(out_buf.at[1, p, r], *odd)
         message(1, p, r).start()
 
+        @pl.when(r == 0)
+        def _():
+            store_message(out_buf.at[0, p, r], *even)
+            message(0, p, r).start()
+
         @pl.when(r > 0)
         def _():
-            arrived(0, p, r - 1)
-            arrived(1, p, r - 1)
-
-        store_message(out_buf.at[0, p, r], *merge([received(0, p, r), received(1, p, r), even]))
-        message(0, p, r).start()
-
-        @pl.when(i == 1)
+            keep(0, p, r, even)
+
+        @pl.when(i == 2)
         def _():
             wait_rows(1)
 
@@ -226,33 +265,29 @@
         even, odd = halves(acc, m_left)
         store_message(out_buf.at[3, p, r], *odd)
         message(3, p, r).start()
-
-        @pl.when(r == 0)
-        def _():
-            own_o[p] = even[0]
-            own_s[p, 0:1] = even[1]
-            own_s[p, 1:2] = even[2]
-
-        @pl.when(r > 0)
-        def _():
-            arrived(3, p, r - 1)
-
-            @pl.when(r > 1)
-            def _():
-                arrived(2, p, r - 1)
-
-            store_message(out_buf.at[2, p, r], *merge([received(2, p, r), received(3, p, r), even]))
-            message(2, p, r).start()
+        keep(1, p, r, even)
+
+        @pl.when(i == 3)
+        def _():
+            pass_on(0, 1)
+
+        @pl.when(i == 5)
+        def _():
+            pass_on(1, 1)
+            pass_on(0, 2)
 
         return m_next
 
     lax.fori_loop(0, PHASES * ROUNDS, body, top)
+    pass_on(1, 2)
+    pass_on(0, 3)
+    pass_on(1, 3)
 
     for p in range(PHASES):
         for kind in range(4):
             arrived(kind, p, ROUNDS - 1)
         parts = [received(kind, p, ROUNDS) for kind in range(4)]
-        parts.append((own_o[p], own_s[p, 0:1], own_s[p, 1:2]))
+        parts.append(kept(1, p, 0))
         o, _, l = merge(parts)
         read = (o / l).T.astype(jnp.bfloat16).astype(jnp.float32)
         result[p] = read
@@ -292,26 +327,38 @@
     span = read_ref.at[:, pl.ds(0, (HEADS - 1) * DH)]
     pltpu.make_async_copy(span, span, r_send).wait()
     pltpu.make_async_copy(span, span, r_recv).wait()
-
-
-def memory_reads(queries, memory_keys, memory_values, probe_blocks, probe_counts):
+    gate = opening[...]
+    near = near_ref[...].astype(jnp.float32)
+    mixed_ref[...] = (gate * read_ref[...] + (1.0 - gate) * near).astype(jnp.bfloat16)
+
+
+def local(queries, local_read, gate_logits, memory_keys, memory_values, probe_blocks, probe_counts):
     vmem = pl.BlockSpec(memory_space=pltpu.VMEM)
-    smem = pl.BlockSpec(memory_space=pltpu.SMEM)
+    hbm = pl.BlockSpec(memory_space=pl.ANY)
     return pl.pallas_call(
         kernel,
-        out_shape=jax.ShapeDtypeStruct((8, HEADS * DH), jnp.float32),
-        in_specs=[smem, smem, vmem, vmem, vmem],
+        out_shape=jax.ShapeDtypeStruct((8, HEADS * DH), jnp.bfloat16),
+        in_specs=[hbm] * 7,
         out_specs=vmem,
         scratch_shapes=[
+            pltpu.SMEM((1, 1, PMAX), jnp.int32),
+            pltpu.SMEM((1, 1), jnp.int32),
+            pltpu.SMEM((HEADS,), jnp.float32),
+            pltpu.VMEM((32, BLOCK, DH), jnp.bfloat16),
+            pltpu.VMEM((32, BLOCK, DH), jnp.bfloat16),
+            pltpu.VMEM((8, HEADS * DH), jnp.bfloat16),
+            pltpu.VMEM((8, HEADS * DH), jnp.float32),
+            pltpu.VMEM((8, HEADS * DH), jnp.float32),
             pltpu.VMEM((PHASES, HEADS * PART, DH), jnp.bfloat16),
             pltpu.VMEM((KEYS, DH), jnp.bfloat16),
             pltpu.VMEM((VROWS, KEYS), jnp.bfloat16),
             pltpu.VMEM((2, KEYS, 2 * CHUNK), jnp.float32),
-            pltpu.VMEM((PHASES, DH, CHUNK), jnp.float32),
-            pltpu.VMEM((PHASES, 8, CHUNK), jnp.float32),
+            pltpu.VMEM((2, PHASES, ROUNDS, DH, CHUNK), jnp.float32),
+            pltpu.VMEM((2, PHASES, ROUNDS, 8, CHUNK), jnp.float32),
             pltpu.VMEM((4, PHASES, ROUNDS, MSG, CHUNK), jnp.bfloat16),
             pltpu.VMEM((4, PHASES, ROUNDS + 1, MSG, CHUNK), jnp.bfloat16),
             pltpu.VMEM((PHASES, CHUNK, DH), jnp.float32),
+            pltpu.SemaphoreType.DMA((PHASES + 6,)),
             pltpu.SemaphoreType.DMA((PHASES,)),
             pltpu.SemaphoreType.DMA((PHASES,)),
             pltpu.SemaphoreType.DMA((4, PHASES, ROUNDS)),
@@ -320,23 +367,18 @@
             pltpu.SemaphoreType.DMA,
         ],
         compiler_params=pltpu.CompilerParams(
-            collective_id=0, has_side_effects=True, vmem_limit_bytes=48 << 20
+            collective_id=0, has_side_effects=True, vmem_limit_bytes=63 << 20
         ),
         name="memory_reads",
     )(
         probe_blocks,
         probe_counts,
+        gate_logits,
         queries,
         memory_keys.reshape(-1, BLOCK, DH),
         memory_values.reshape(-1, BLOCK, DH),
+        local_read,
     )
-
-
-def local(queries, local_read, gate_logits, memory_keys, memory_values, probe_blocks, probe_counts):
-    reads = memory_reads(queries, memory_keys, memory_values, probe_blocks, probe_counts)
-    opening = jnp.repeat(jax.nn.sigmoid(gate_logits), DH)
-    mixed = opening * reads + (1.0 - opening) * local_read.astype(jnp.float32)
-    return mixed.astype(jnp.bfloat16)
 
 
 def solution(mesh):

time: 65.7 us -> 59.4 us (0.904)
  local copies, waits for them, and re-layouts: 4.99 us -> 1.47 us
  Pallas kernels: 59 us -> 57.1 us
  other arithmetic: 0.74 us -> 0 us
    unnamed x12 -> x1, local copies, waits for them, and re-layouts: 4.92 us -> 1.47 us
    pallas_call x1, Pallas kernels: 59 us -> 57.1 us  [local(): pl.pallas_call(kernel, out_shape=jax.ShapeDtypeStruct((8, HEADS * DH), jn...]
where the time goes in v2:
time: 59.4 us; the launch traced here: 59.3 us
  Pallas kernels  57.1 us (96%)
  local copies, waits for them, and re-layouts  1.47 us (2%)
  between operations  0.66 us (1%)
    pallas_call x1, Pallas kernels, local(): pl.pallas_call(kernel, out_shape=jax.ShapeDtypeStruct((8, HEADS * DH), jn...  57.1 us
    unnamed x1, local copies, waits for them, and re-layouts  1.47 us

profile of v2, /device:TPU:7, one launch (start us, length us, event | category | flops | bytes accessed | tf_op | source)
XLA Modules:
  0.0 59.3 jit_solution(2880895904357914812)
XLA Ops:
  0.7 57.1 %memory_reads.1 = bf16[8,4096]{1,0:T(8,128)(2,1)} custom-call(s32[1,1,16]{2,1,0:T(1,128)} %blocks_hbm.1, s32[1,1]{1,0:T(1,128)S(6)} %copy.9.count_hbm, f32[32]{0:T(128)} %gate_hbm.1, bf16[128,4096]{1,0:T(8,128)(2,1)} %q_ref.1, bf16[32,128,128]{2,1,0:T(8,128)(2,1)} %bitcast.2, bf16[32,128,128]{2,1,0:T(8,128)(2,1)} %bitcast.3, bf16[8,4096]{1,0:T(8,128)(2,1)} %near_hbm.1), custom_call_target="tpu_custom_call" | custom-call | tf_op jit(solution)/shard_map/memory_reads/pallas_call | solution.py:338
  57.8 1.5 %copy.10 = bf16[8,4096]{1,0:T(8,128)(2,1)} copy(bf16[8,4096]{1,0:T(8,128)(2,1)} %memory_reads.1) | data formatting | bytes 131072

commit v3 on v2

--- a/solution.py
+++ b/solution.py
@@ -23,35 +23,10 @@
 CHUNK = 2 * PART
 TILE = 256
 VROWS = 144
-MSG = 144
 
 
 def add(a, b):
     return b if a is None else a + b
-
-
-def load_message(ref):
-    o = ref[0:DH, :].astype(jnp.float32)
-    stats = ref[DH:MSG, :].astype(jnp.float32)
-    m = stats[0:1] + stats[1:2] + stats[2:3]
-    l = stats[3:4] + stats[4:5] + stats[5:6]
-    return o, m, l
-
-
-def pieces(x):
-    hi = x.astype(jnp.bfloat16).astype(jnp.float32)
-    rest = x - hi
-    mid = rest.astype(jnp.bfloat16).astype(jnp.float32)
-    return hi, mid, rest - mid
-
-
-def store_message(ref, o, m, l):
-    ref[0:DH, :] = o.astype(ref.dtype)
-    row = lax.broadcasted_iota(jnp.int32, (MSG - DH, CHUNK), 0)
-    stats = jnp.zeros((MSG - DH, CHUNK), jnp.float32)
-    for i, piece in enumerate(pieces(m) + pieces(l)):
-        stats = jnp.where(row == i, piece, stats)
-    ref[DH:MSG, :] = stats.astype(ref.dtype)
 
 
 def merge(parts):
@@ -69,8 +44,8 @@
 def kernel(
     blocks_hbm, count_hbm, gate_hbm, q_ref, k_hbm, v_hbm, near_hbm, mixed_ref,
     blocks_ref, count_ref, gate_ref, k_ref, v_ref, near_ref, opening, read_ref,
-    qa, kp, vt, scores, part_o, part_s, out_buf, in_buf, result,
-    load_sem, q_send, q_recv, m_send, m_recv, r_send, r_recv,
+    qa, kp, vt, scores, part_o, part_s, out_o, out_s, in_o, in_s, result,
+    load_sem, q_send, q_recv, m_send, m_recv, s_send, s_recv, r_send, r_recv,
 ):
     g = lax.axis_index("index")
     h = lax.axis_index("head")
@@ -116,7 +91,12 @@
     for p in range(PHASES):
 
         def send_rows(i, _):
-            to = lax.rem(h + i, HEADS)
+            s, t = lax.rem(i, 4), lax.div(i, 8)
+            dx = 1 + 2 * s - 3 * lax.div(s, 2)
+            dy = 2 - t + 3 * lax.div(t, 2) - 2 * lax.div(t, 3)
+            x, y = lax.rem(lax.div(h, 8) + dx, 4), lax.rem(lax.rem(lax.div(h, 2), 4) + dy, 4)
+            to = 8 * x + 2 * y + lax.rem(lax.rem(h, 2) + lax.rem(lax.div(i, 4), 2), 2)
+
             pltpu.make_async_remote_copy(
                 src_ref=q_ref.at[pl.ds(p * PART, PART), pl.ds(pl.multiple_of(to * DH, DH), DH)],
                 dst_ref=qa.at[p, pl.ds(pl.multiple_of(h * PART, PART), PART), :],
@@ -127,7 +107,8 @@
             ).start()
             return 0
 
-        lax.fori_loop(1, HEADS, send_rows, 0)
+        lax.fori_loop(0, 27, send_rows, 0)
+        lax.fori_loop(28, HEADS, send_rows, 0)
 
     def wait_rows(p):
         own_rows[p].wait()
@@ -155,18 +136,34 @@
 
     hop = (2, 1, -2, -1)
 
-    def message(kind, p, r):
-        return pltpu.make_async_remote_copy(
-            src_ref=out_buf.at[kind, p, r],
-            dst_ref=in_buf.at[kind, p, r + 1],
-            send_sem=m_send.at[kind, p, r],
-            recv_sem=m_recv.at[kind, p, r],
-            device_id=(plane(hop[kind]), h),
-            device_id_type=MESH,
-        )
-
-    def arrived(kind, p, r):
-        message(kind, p, r).wait_recv()
+    def message(kind, p, r, step=None):
+        to = plane(hop[kind] if step is None else step)
+        return [
+            pltpu.make_async_remote_copy(
+                src_ref=src, dst_ref=dst, send_sem=send, recv_sem=recv, device_id=(to, h), device_id_type=MESH
+            )
+            for src, dst, send, recv in (
+                (
+                    out_s.at[kind, p, r, pl.ds(0, 2)],
+                    in_s.at[kind, p, r, pl.ds(0, 2)],
+                    s_send.at[kind, p, r],
+                    s_recv.at[kind, p, r],
+                ),
+                (out_o.at[kind, p, r], in_o.at[kind, p, r], m_send.at[kind, p, r], m_recv.at[kind, p, r]),
+            )
+        ]
+
+    def send(kind, p, r, part, step=None):
+        out_o[kind, p, r] = part[0].astype(jnp.bfloat16)
+        out_s[kind, p, r, 0:1] = part[1]
+        out_s[kind, p, r, 1:2] = part[2]
+        for copy in message(kind, p, r, step):
+            copy.start()
+
+    def receive(kind, p, r):
+        for copy in message(kind, p, r):
+            copy.wait_recv()
+        return in_o[kind, p, r].astype(jnp.float32), in_s[kind, p, r, 0:1], in_s[kind, p, r, 1:2]
 
     def from_step(i, a):
         return lax.div(i + (8 - a), 8)
@@ -210,9 +207,6 @@
         odd = (acc[0:DH, CHUNK:], m[:, CHUNK:], acc[DH : DH + 1, CHUNK:])
         return even, odd
 
-    def received(kind, p, slot):
-        return load_message(in_buf.at[kind, p, slot])
-
     wait_rows(0)
     q = right_rows(0, 0)
     top = None
@@ -232,61 +226,61 @@
     def pass_on(p, r):
         for side in range(2):
             parts = [kept(side, p, r)]
-            for kind in (2 * side, 2 * side + 1):
-                if kind == 2 and r == 1:
-                    continue
-                arrived(kind, p, r - 1)
-                parts.append(received(kind, p, r))
-            store_message(out_buf.at[2 * side, p, r], *merge(parts))
-            message(2 * side, p, r).start()
+            if r > 1 or (side == 0 and p == 1):
+                parts.append(receive(2 * side, p, r - 1))
+            parts.append(receive(2 * side + 1, p, r - 1))
+            send(2 * side, p, r, merge(parts))
 
     def body(i, m_right):
         p, r = schedule(i)
         acc, m_left = unit(left_rows(p, r), m_right, 0)
         even, odd = halves(acc, m_right)
-        store_message(out_buf.at[1, p, r], *odd)
-        message(1, p, r).start()
 
         @pl.when(r == 0)
         def _():
-            store_message(out_buf.at[0, p, r], *even)
-            message(0, p, r).start()
+            send(0, p, r, even, 1 + p)
 
         @pl.when(r > 0)
         def _():
             keep(0, p, r, even)
 
+        @pl.when(i == 0)
+        def _():
+            keep(0, 0, 0, odd)
+
+        @pl.when(i > 0)
+        def _():
+            send(1, p, r, odd)
+
         @pl.when(i == 2)
         def _():
+            send(1, 0, 0, merge([kept(0, 0, 0), receive(0, 0, 0)]))
             wait_rows(1)
 
         pn, rn = schedule(i + 1 - lax.div(i + 1, 8))
         acc, m_next = unit(right_rows(pn, rn), m_left, 1)
         even, odd = halves(acc, m_left)
-        store_message(out_buf.at[3, p, r], *odd)
-        message(3, p, r).start()
+        send(3, p, r, odd)
         keep(1, p, r, even)
 
-        @pl.when(i == 3)
+        @pl.when(i == 4)
         def _():
             pass_on(0, 1)
 
         @pl.when(i == 5)
         def _():
             pass_on(1, 1)
-            pass_on(0, 2)
 
         return m_next
 
     lax.fori_loop(0, PHASES * ROUNDS, body, top)
+    pass_on(0, 2)
     pass_on(1, 2)
     pass_on(0, 3)
     pass_on(1, 3)
 
     for p in range(PHASES):
-        for kind in range(4):
-            arrived(kind, p, ROUNDS - 1)
-        parts = [received(kind, p, ROUNDS) for kind in range(4)]
+        parts = [receive(kind, p, ROUNDS - 1) for kind in range(4)]
         parts.append(kept(1, p, 0))
         o, _, l = merge(parts)
         read = (o / l).T.astype(jnp.bfloat16).astype(jnp.float32)
@@ -323,7 +317,8 @@
             for r in range(ROUNDS):
                 if kind == 2 and r == 0:
                     continue
-                message(kind, p, r).wait_send()
+                for copy in message(kind, p, r):
+                    copy.wait_send()
     span = read_ref.at[:, pl.ds(0, (HEADS - 1) * DH)]
     pltpu.make_async_copy(span, span, r_send).wait()
     pltpu.make_async_copy(span, span, r_recv).wait()
@@ -355,12 +350,16 @@
             pltpu.VMEM((2, KEYS, 2 * CHUNK), jnp.float32),
             pltpu.VMEM((2, PHASES, ROUNDS, DH, CHUNK), jnp.float32),
             pltpu.VMEM((2, PHASES, ROUNDS, 8, CHUNK), jnp.float32),
-            pltpu.VMEM((4, PHASES, ROUNDS, MSG, CHUNK), jnp.bfloat16),
-            pltpu.VMEM((4, PHASES, ROUNDS + 1, MSG, CHUNK), jnp.bfloat16),
+            pltpu.VMEM((4, PHASES, ROUNDS, DH, CHUNK), jnp.bfloat16),
+            pltpu.VMEM((4, PHASES, ROUNDS, 8, CHUNK), jnp.float32),
+            pltpu.VMEM((4, PHASES, ROUNDS, DH, CHUNK), jnp.bfloat16),
+            pltpu.VMEM((4, PHASES, ROUNDS, 8, CHUNK), jnp.float32),
             pltpu.VMEM((PHASES, CHUNK, DH), jnp.float32),
             pltpu.SemaphoreType.DMA((PHASES + 6,)),
             pltpu.SemaphoreType.DMA((PHASES,)),
             pltpu.SemaphoreType.DMA((PHASES,)),
+            pltpu.SemaphoreType.DMA((4, PHASES, ROUNDS)),
+            pltpu.SemaphoreType.DMA((4, PHASES, ROUNDS)),
             pltpu.SemaphoreType.DMA((4, PHASES, ROUNDS)),
             pltpu.SemaphoreType.DMA((4, PHASES, ROUNDS)),
             pltpu.SemaphoreType.DMA,

time: 59.4 us -> 57.4 us (0.966); the launches traced: 59.3 us -> 56.4 us
  Pallas kernels: 57.1 us -> 54.3 us
    pallas_call x1, Pallas kernels: 57.1 us -> 54.3 us  [local(): pl.pallas_call(kernel, out_shape=jax.ShapeDtypeStruct((8, HEADS * DH), jn...]
where the time goes in v3:
time: 57.4 us; the launch traced here: 56.4 us
  Pallas kernels  54.3 us (95%)
  local copies, waits for them, and re-layouts  1.47 us (3%)
  between operations  0.66 us (1%)
    pallas_call x1, Pallas kernels, local(): pl.pallas_call(kernel, out_shape=jax.ShapeDtypeStruct((8, HEADS * DH), jn...  54.3 us
    unnamed x1, local copies, waits for them, and re-layouts  1.47 us

profile of v3, /device:TPU:7, one launch (start us, length us, event | category | flops | bytes accessed | tf_op | source)
XLA Modules:
  0.0 56.4 jit_solution(441456730224329168)
XLA Ops:
  0.7 54.3 %memory_reads.1 = bf16[8,4096]{1,0:T(8,128)(2,1)} custom-call(s32[1,1,16]{2,1,0:T(1,128)} %blocks_hbm.1, s32[1,1]{1,0:T(1,128)S(6)} %copy.9.count_hbm, f32[32]{0:T(128)} %gate_hbm.1, bf16[128,4096]{1,0:T(8,128)(2,1)} %q_ref.1, bf16[32,128,128]{2,1,0:T(8,128)(2,1)} %bitcast.2, bf16[32,128,128]{2,1,0:T(8,128)(2,1)} %bitcast.3, bf16[8,4096]{1,0:T(8,128)(2,1)} %near_hbm.1), custom_call_target="tpu_custom_call" | custom-call | tf_op jit(solution)/shard_map/memory_reads/pallas_call | solution.py:333
  54.9 1.5 %copy.10 = bf16[8,4096]{1,0:T(8,128)(2,1)} copy(bf16[8,4096]{1,0:T(8,128)(2,1)} %memory_reads.1) | data formatting | bytes 131072

commit v4 on v3

--- a/solution.py
+++ b/solution.py
@@ -17,10 +17,11 @@
 SCALE = DH ** -0.5 * math.log2(math.e)
 MESH = pl.DeviceIdType.MESH
 
-PHASES = 2
+PHASES = 4
 ROUNDS = 4
 PART = 128 // PHASES
 CHUNK = 2 * PART
+FOLD = 2 * CHUNK
 TILE = 256
 VROWS = 144
 
@@ -165,30 +166,34 @@
             copy.wait_recv()
         return in_o[kind, p, r].astype(jnp.float32), in_s[kind, p, r, 0:1], in_s[kind, p, r, 1:2]
 
-    def from_step(i, a):
-        return lax.div(i + (8 - a), 8)
-
-    def schedule(i):
-        p = from_step(i, 3) - from_step(i, 5) + from_step(i, 6)
-        r = i - 3 * from_step(i, 3) + from_step(i, 5) - 2 * from_step(i, 6)
+    units = (
+        (0, 0), (0, 1), (0, 2), (1, 0), (1, 1), (2, 0), (1, 2), (3, 0),
+        (2, 1), (3, 1), (0, 3), (2, 2), (3, 2), (1, 3), (2, 3), (3, 3),
+    )
+
+    def schedule(u):
+        p = r = 0
+        for a in range(1, len(units)):
+            on = lax.div(u + (len(units) - a), len(units))
+            p = p + (units[a][0] - units[a - 1][0]) * on
+            r = r + (units[a][1] - units[a - 1][1]) * on
         return p, r
 
     def rows_of(p, step):
         return qa[p, pl.ds(pl.multiple_of(plane(step) * CHUNK, CHUNK), CHUNK), :]
 
-    def right_rows(p, r):
-        return jnp.concatenate([rows_of(p, 8 - 2 * r), rows_of(p, 7 - 2 * r)], axis=0)
-
-    def left_rows(p, r):
-        even = (8 - 2 * r) * lax.div(r + 3, 4)
-        return jnp.concatenate([rows_of(p, -even), rows_of(p, 2 * r - 7)], axis=0)
+    def unit_rows(u):
+        p, r = schedule(u)
+        own = (8 - 2 * r) * lax.div(r + 3, 4)
+        steps = (8 - 2 * r, 7 - 2 * r, -own, 2 * r - 7)
+        return jnp.concatenate([rows_of(p, step) for step in steps], axis=0)
 
     def score_tile(q, slot, k):
         s = lax.dot_general(
             kp[k : k + TILE, :], q, (((1,), (1,)), ((), ())), preferred_element_type=jnp.float32
         )
         scores[slot, k : k + TILE, :] = s
-        return jnp.max(s.reshape(TILE // 8, 8, 2 * CHUNK), axis=0)
+        return jnp.max(s.reshape(TILE // 8, 8, 4 * CHUNK), axis=0)
 
     def value_tile(slot, m, k):
         w = jnp.exp2((scores[slot, k : k + TILE, :] - m) * SCALE).astype(jnp.bfloat16)
@@ -202,13 +207,23 @@
             acc = add(acc, value_tile(slot, m, k))
         return acc, jnp.max(top, axis=0, keepdims=True)
 
-    def halves(acc, m):
-        even = (acc[0:DH, 0:CHUNK], m[:, 0:CHUNK], acc[DH : DH + 1, 0:CHUNK])
-        odd = (acc[0:DH, CHUNK:], m[:, CHUNK:], acc[DH : DH + 1, CHUNK:])
+    left_lanes = lax.broadcasted_iota(jnp.int32, (DH // 2, FOLD), 1) < CHUNK
+    left_line = lax.broadcasted_iota(jnp.int32, (8, FOLD), 1) < CHUNK
+
+    def folded(acc, m, side):
+        lanes = slice(side * FOLD, (side + 1) * FOLD)
+        upper, lower = acc[0 : DH // 2, lanes], acc[DH // 2 : DH, lanes]
+        even = [jnp.where(left_lanes, upper, pltpu.roll(lower, CHUNK, 1))]
+        odd = [jnp.where(left_lanes, pltpu.roll(upper, CHUNK, 1), lower)]
+        for line in (m[:, lanes], acc[DH : DH + 1, lanes]):
+            line = jnp.broadcast_to(line, (8, FOLD))
+            other = pltpu.roll(line, CHUNK, 1)
+            even.append(jnp.where(left_line, line, other)[0:1])
+            odd.append(jnp.where(left_line, other, line)[0:1])
         return even, odd
 
     wait_rows(0)
-    q = right_rows(0, 0)
+    q = unit_rows(0)
     top = None
     for k in range(0, KEYS, TILE):
         t = score_tile(q, 0, k)
@@ -223,71 +238,86 @@
     def kept(side, p, r):
         return part_o[side, p, r], part_s[side, p, r, 0:1], part_s[side, p, r, 1:2]
 
+    def pass_seven(p):
+        send(1, p, 0, merge([kept(0, p, 0), receive(0, p, 0)]))
+
     def pass_on(p, r):
         for side in range(2):
             parts = [kept(side, p, r)]
-            if r > 1 or (side == 0 and p == 1):
+            if r > 1 or (side == 0 and p > 1):
                 parts.append(receive(2 * side, p, r - 1))
             parts.append(receive(2 * side + 1, p, r - 1))
             send(2 * side, p, r, merge(parts))
 
-    def body(i, m_right):
-        p, r = schedule(i)
-        acc, m_left = unit(left_rows(p, r), m_right, 0)
-        even, odd = halves(acc, m_right)
+    def finish(u, acc, m):
+        p, r = schedule(u)
+        even, odd = folded(acc, m, 0)
 
         @pl.when(r == 0)
         def _():
-            send(0, p, r, even, 1 + p)
+            send(0, p, r, even, 1 + lax.div(p, 2))
 
         @pl.when(r > 0)
         def _():
             keep(0, p, r, even)
 
-        @pl.when(i == 0)
+        waits = jnp.logical_and(r == 0, p < 2)
+
+        @pl.when(waits)
         def _():
-            keep(0, 0, 0, odd)
-
-        @pl.when(i > 0)
+            keep(0, p, 0, odd)
+
+        @pl.when(jnp.logical_not(waits))
         def _():
             send(1, p, r, odd)
 
-        @pl.when(i == 2)
-        def _():
-            send(1, 0, 0, merge([kept(0, 0, 0), receive(0, 0, 0)]))
-            wait_rows(1)
-
-        pn, rn = schedule(i + 1 - lax.div(i + 1, 8))
-        acc, m_next = unit(right_rows(pn, rn), m_left, 1)
-        even, odd = halves(acc, m_left)
+        even, odd = folded(acc, m, 1)
         send(3, p, r, odd)
         keep(1, p, r, even)
 
-        @pl.when(i == 4)
-        def _():
-            pass_on(0, 1)
-
-        @pl.when(i == 5)
-        def _():
-            pass_on(1, 1)
-
-        return m_next
-
-    lax.fori_loop(0, PHASES * ROUNDS, body, top)
-    pass_on(0, 2)
-    pass_on(1, 2)
-    pass_on(0, 3)
-    pass_on(1, 3)
-
-    for p in range(PHASES):
+    def body(i, m):
+        for p in range(1, PHASES):
+
+            @pl.when(i == p)
+            def _():
+                if p == 3:
+                    pass_seven(1)
+                wait_rows(p)
+
+        acc, m_next = unit(unit_rows(2 * i + 1), m, 0)
+        finish(2 * i, acc, m)
+        acc, m = unit(unit_rows(2 * i + 2 - lax.div(i, 7)), m_next, 1)
+        finish(2 * i + 1, acc, m_next)
+        for at, hops in (
+            (1, ((0, 0),)),
+            (3, ((0, 1),)),
+            (4, ((1, 1), (2, 1))),
+            (5, ((0, 2), (3, 1))),
+            (6, ((1, 2), (2, 2))),
+        ):
+
+            @pl.when(i == at)
+            def _():
+                for p, r in hops:
+                    if r:
+                        pass_on(p, r)
+                    else:
+                        pass_seven(p)
+
+        return m
+
+    lax.fori_loop(0, PHASES * ROUNDS // 2, body, top)
+
+    def give_back(p):
         parts = [receive(kind, p, ROUNDS - 1) for kind in range(4)]
         parts.append(kept(1, p, 0))
         o, _, l = merge(parts)
-        read = (o / l).T.astype(jnp.bfloat16).astype(jnp.float32)
-        result[p] = read
+        turned = jnp.concatenate([o / l] * 2, axis=0).T
+        read = jnp.where(left_lanes, turned[0:CHUNK], turned[CHUNK:])
+        result[p] = read.astype(jnp.bfloat16).astype(jnp.float32)
 
         def give(b, _):
-            to = lax.div(b, 8) * 16 + 8 * p + lax.rem(b, 8)
+            to = lax.div(b, 4) * 16 + 4 * p + lax.rem(b, 4)
 
             @pl.when(to != h)
             def _():
@@ -308,7 +338,17 @@
 
             return 0
 
-        lax.fori_loop(0, 16, give, 0)
+        lax.fori_loop(0, 8, give, 0)
+
+    pass_on(0, 3)
+    pass_on(3, 2)
+    pass_on(1, 3)
+    pass_on(2, 3)
+    give_back(0)
+    pass_on(3, 3)
+    give_back(1)
+    give_back(2)
+    give_back(3)
 
     for p in range(PHASES):
         part = qa.at[p, pl.ds(0, (HEADS - 1) * PART), :]
@@ -347,13 +387,13 @@
             pltpu.VMEM((PHASES, HEADS * PART, DH), jnp.bfloat16),
             pltpu.VMEM((KEYS, DH), jnp.bfloat16),
             pltpu.VMEM((VROWS, KEYS), jnp.bfloat16),
-            pltpu.VMEM((2, KEYS, 2 * CHUNK), jnp.float32),
-            pltpu.VMEM((2, PHASES, ROUNDS, DH, CHUNK), jnp.float32),
-            pltpu.VMEM((2, PHASES, ROUNDS, 8, CHUNK), jnp.float32),
-            pltpu.VMEM((4, PHASES, ROUNDS, DH, CHUNK), jnp.bfloat16),
-            pltpu.VMEM((4, PHASES, ROUNDS, 8, CHUNK), jnp.float32),
-            pltpu.VMEM((4, PHASES, ROUNDS, DH, CHUNK), jnp.bfloat16),
-            pltpu.VMEM((4, PHASES, ROUNDS, 8, CHUNK), jnp.float32),
+            pltpu.VMEM((2, KEYS, 4 * CHUNK), jnp.float32),
+            pltpu.VMEM((2, PHASES, ROUNDS, DH // 2, FOLD), jnp.float32),
+            pltpu.VMEM((2, PHASES, ROUNDS, 8, FOLD), jnp.float32),
+            pltpu.VMEM((4, PHASES, ROUNDS, DH // 2, FOLD), jnp.bfloat16),
+            pltpu.VMEM((4, PHASES, ROUNDS, 8, FOLD), jnp.float32),
+            pltpu.VMEM((4, PHASES, ROUNDS, DH // 2, FOLD), jnp.bfloat16),
+            pltpu.VMEM((4, PHASES, ROUNDS, 8, FOLD), jnp.float32),
             pltpu.VMEM((PHASES, CHUNK, DH), jnp.float32),
             pltpu.SemaphoreType.DMA((PHASES + 6,)),
             pltpu.SemaphoreType.DMA((PHASES,)),

time: 57.4 us -> 57 us (level)
  the two profiles are of different devices: /device:TPU:7 before, /device:TPU:31 now
where the time goes in v4:
time: 57 us; the launch traced here: 56.9 us
  Pallas kernels  54.7 us (96%)
  local copies, waits for them, and re-layouts  1.47 us (3%)
  between operations  0.66 us (1%)
    pallas_call x1, Pallas kernels, local(): pl.pallas_call(kernel, out_shape=jax.ShapeDtypeStruct((8, HEADS * DH), jn...  54.7 us
    unnamed x1, local copies, waits for them, and re-layouts  1.47 us

profile of v4, /device:TPU:31, one launch (start us, length us, event | category | flops | bytes accessed | tf_op | source)
XLA Modules:
  0.0 56.9 jit_solution(4844070529023977225)
XLA Ops:
  0.7 54.7 %memory_reads.1 = bf16[8,4096]{1,0:T(8,128)(2,1)} custom-call(s32[1,1,16]{2,1,0:T(1,128)} %blocks_hbm.1, s32[1,1]{1,0:T(1,128)S(6)} %copy.9.count_hbm, f32[32]{0:T(128)} %gate_hbm.1, bf16[128,4096]{1,0:T(8,128)(2,1)} %q_ref.1, bf16[32,128,128]{2,1,0:T(8,128)(2,1)} %bitcast.2, bf16[32,128,128]{2,1,0:T(8,128)(2,1)} %bitcast.3, bf16[8,4096]{1,0:T(8,128)(2,1)} %near_hbm.1), custom_call_target="tpu_custom_call" | custom-call | tf_op jit(solution)/shard_map/memory_reads/pallas_call | solution.py:373
  55.4 1.5 %copy.10 = bf16[8,4096]{1,0:T(8,128)(2,1)} copy(bf16[8,4096]{1,0:T(8,128)(2,1)} %memory_reads.1) | data formatting | bytes 131072
